TPU v7x, 32 devices: a whole 2x2x4 slice. The times are simulated.
32 devices in a mesh: grp: 4 (over y, core), idx: 8 (over z, x).
Axes of the slice: x: 2, y: 2, z: 4, core: 2. Of those that a mesh axis runs over, the one named last changes fastest.
Arguments:
- queries: bfloat16 [8, 1024, 768], P('idx', 'grp'), may hold values from -6 to 6
- passages: bfloat16 [8, 1024, 768], P('idx', 'grp'), may hold values from -6 to 6
- partner: int32 [2, 8], replicated, may hold values from 0 to 7, each once within a row
- pair_codes: int32 [2, 8, 4, 16], P(None, None, 'grp'), may hold values from 0 to 15, as said below
- pair_count: int32 [2, 8, 4], P(None, None, 'grp'), may hold values from 4 to 16, as said below
- positive: int32 [8, 1024], P('idx', 'grp'), may hold values from 0 to 1023
Outputs:
- query_grad: float32 [8, 1024, 768], P('idx', 'grp')
- passage_grad: float32 [8, 1024, 768], P('idx', 'grp')
Inputs may be any that keep to these rules, and one draw needn't show every extreme that they name: Each row of partner is a permutation of the clusters: in round r the queries of cluster c are scored against the panel of cluster partner[r, c]. `pair_codes`: the 16 codes of one list are distinct. `pair_count`: in every round at least one list has all 16 slots live.
All inputs are finite; a program needn't handle non-finite values.
Results may differ from a plain program's by a relative error of at most 0.0034.
Values may be sent and summed in bfloat16 or wider, within the bound.
A program may use at most 128 MiB of HBM per device.

v0:
```python
import math

import jax
import jax.numpy as jnp
from jax import lax
from jax.sharding import PartitionSpec as P

BLK = 128


positive_weight = 16.0


def score_list(query_set, panel_shard, pair_list, live_count, logit_scale):
    query_tiles = query_set.shape[0] // BLK
    panel_tiles = panel_shard.shape[0] // BLK
    columns = query_set.shape[1]
    slot_total = pair_list.shape[0]
    group_size = math.gcd(48, slot_total)
    query_grid = query_set.reshape(query_tiles, BLK, columns)
    panel_grid = panel_shard.reshape(panel_tiles, BLK, columns)

    def one_group(turn_index, partial_sums):
        query_acc, panel_acc = partial_sums
        first_slot = turn_index * group_size
        live_mask = first_slot + jnp.arange(group_size, dtype=jnp.int32) < live_count
        query_index = pair_list // panel_tiles
        panel_index = pair_list % panel_tiles
        query_block_list = jnp.take(query_grid, query_index, axis=0)
        panel_block_list = jnp.take(panel_grid, panel_index, axis=0)
        similarity_scores = logit_scale * jnp.einsum(
            "wzr,wlr->wzl", query_block_list, panel_block_list, preferred_element_type=jnp.float32
        )
        sample_weights = jnp.where(
            live_mask[:, None, None], jax.nn.sigmoid(similarity_scores), 0.0
        ).astype(jnp.bfloat16)
        query_portion = jnp.einsum(
            "nku,nua->nka", sample_weights, panel_block_list, preferred_element_type=jnp.float32
        )
        panel_portion = jnp.einsum(
            "swc,swj->scj", sample_weights, query_block_list, preferred_element_type=jnp.float32
        )
        query_acc = query_acc + jax.ops.segment_sum(
            query_portion, query_index, num_segments=query_tiles
        )
        panel_acc = panel_acc + jax.ops.segment_sum(
            panel_portion, panel_index, num_segments=panel_tiles
        )
        return (query_acc, panel_acc)

    start_sums = (
        jnp.zeros(query_grid.shape, jnp.float32),
        jnp.zeros(panel_grid.shape, jnp.float32),
    )
    turn_total = slot_total // group_size
    query_acc, panel_acc = lax.fori_loop(0, turn_total, one_group, start_sums)
    return (
        logit_scale * query_acc.reshape(query_set.shape),
        logit_scale * panel_acc.reshape(panel_shard.shape),
    )


def near_terms(query_set, targets, own_panel, row_offset, logit_scale):
    row_total = own_panel.shape[0]
    local_rows = targets - row_offset
    owned = (local_rows >= 0) & (local_rows < row_total)
    safe_rows = jnp.clip(local_rows, 0, row_total - 1)
    target_rows = jnp.take(own_panel, safe_rows, axis=0).astype(jnp.float32)
    similarity_scores = logit_scale * jnp.sum(query_set.astype(jnp.float32) * target_rows, axis=1)
    factor = jnp.where(owned, positive_weight * (jax.nn.sigmoid(similarity_scores) - 1.0), 0.0)
    query_near = logit_scale * factor[:, None] * target_rows
    panel_near = logit_scale * jax.ops.segment_sum(
        factor[:, None] * query_set.astype(jnp.float32), safe_rows, num_segments=row_total
    )
    return (query_near, panel_near)


def shards(queries, passages, partner, pair_codes, pair_count, positive):
    idx_total = lax.axis_size("idx")
    own_index = lax.axis_index("idx")
    member = lax.axis_index("grp")
    panel_rows = passages.shape[1]
    columns = queries.shape[2]
    pass_total = partner.shape[0]
    logit_scale = columns ** (-0.5)
    inverse = jnp.argsort(partner, axis=1)
    home_queries, home_targets = (
        lax.all_gather(queries, "grp", axis=1, tiled=True),
        lax.all_gather(positive, "grp", axis=1, tiled=True),
    )
    home_set = home_queries[0]
    own_panel = passages[0]
    near_query, near_passage = near_terms(
        home_set, home_targets[0], own_panel, member * panel_rows, logit_scale
    )
    piece_rows = panel_rows // idx_total
    spread = lax.all_to_all(
        own_panel.reshape(idx_total, piece_rows, columns),
        "idx",
        split_axis=0,
        concat_axis=0,
        tiled=True,
    )
    routed = lax.all_to_all(
        jnp.take(spread, partner, axis=0), "idx", split_axis=1, concat_axis=1, tiled=True
    )
    query_acc = near_query
    returned = jnp.zeros((idx_total, piece_rows, columns), jnp.float32)
    for pass_index in range(pass_total):
        query_portion, panel_portion = score_list(
            home_set,
            routed[pass_index].reshape(panel_rows, columns),
            pair_codes[pass_index, own_index, 0],
            pair_count[pass_index, own_index, 0],
            logit_scale,
        )
        query_acc = query_acc + query_portion
        outgoing = panel_portion.astype(jnp.bfloat16).reshape(idx_total, piece_rows, columns)
        arrived = lax.all_to_all(outgoing, "idx", split_axis=0, concat_axis=0, tiled=True)
        returned = returned + jnp.take(arrived, inverse[pass_index], axis=0).astype(jnp.float32)
    far_passage = lax.all_to_all(returned, "idx", split_axis=0, concat_axis=0, tiled=True)
    passage_total = far_passage.reshape(panel_rows, columns) + near_passage
    query_total = lax.psum_scatter(query_acc[None], "grp", scatter_dimension=1, tiled=True)
    return (query_total, passage_total[None])


def solution(mesh):
    in_specs = (
        P("idx", "grp", None),
        P("idx", "grp", None),
        P(),
        P(None, None, "grp", None),
        P(None, None, "grp"),
        P("idx", "grp"),
    )
    out_specs = (P("idx", "grp", None), P("idx", "grp", None))
    return jax.shard_map(shards, mesh=mesh, in_specs=in_specs, out_specs=out_specs, check_vma=False)
```

profile of v0, /device:TPU:0, one launch (start us, length us, event | category | flops | bytes accessed | tf_op | source)
XLA Modules:
  0.0 209.5 jit_solution(2311617937222086063)
XLA Ops:
  7.9 7.3 %all-to-all-start = ((bf16[8,32,768]{2,1,0:T(8,128)(2,1)}), bf16[8,32,768]{2,1,0:T(8,128)(2,1)S(1)}, u32[]{:S(2)}, u32[]{:S(2)}) async-start(bf16[8,32,768]{2,1,0:T(8,128)(2,1)} %bitcast.120), calls=%async_computation | async-start | bytes 786432 | tf_op jit(solution)/shard_map/all_to_all | solution.py:97
  17.8 5.3 %all_gather.6 = s32[1,1024]{1,0:T(1,128)S(1)} all-gather(s32[1,256]{1,0:T(1,128)} %param.17), channel_id=1, replica_groups=mesh['grp'=4,'idx'=8] {'grp'}, dimensions={1}, use_global_device_ids=true | all-gather | bytes 5120 | tf_op jit(solution)/shard_map/all_gather | solution.py:89
  23.8 3.0 %all-to-all-done = bf16[8,32,768]{2,1,0:T(8,128)(2,1)S(1)} async-done(((bf16[8,32,768]{2,1,0:T(8,128)(2,1)}), bf16[8,32,768]{2,1,0:T(8,128)(2,1)S(1)}, u32[]{:S(2)}, u32[]{:S(2)}) %all-to-all-start) | async-done | bytes 393248 | tf_op jit(solution)/shard_map/all_to_all | solution.py:97
  28.5 3.6 %all-to-all-start.1 = ((bf16[2,8,32,768]{3,2,0,1:T(8,128)(2,1)}), bf16[2,8,32,768]{3,2,0,1:T(8,128)(2,1)S(1)}, u32[]{:S(2)}, u32[]{:S(2)}) async-start(bf16[2,8,32,768]{3,2,0,1:T(8,128)(2,1)} %copy.20), calls=%async_computation.1 | async-start | bytes 1572864 | tf_op jit(solution)/shard_map/all_to_all | solution.py:104
  32.9 4.0 %gather_fusion = bf16[1024,768]{1,0:T(8,128)(2,1)S(1)} fusion(bf16[256,768]{1,0:T(8,128)(2,1)S(1)} %bitcast.121, s32[1024]{0:T(1024)S(1)} %broadcast_clamp_fusion), kind=kCustom, calls=%fused_computation.6 | custom fusion | bytes 3149824 | tf_op jit(solution)/shard_map/jit(_take)/gather | solution.py:68
  37.7 14.5 %all-to-all-done.1 = bf16[2,8,32,768]{3,2,0,1:T(8,128)(2,1)S(1)} async-done(((bf16[2,8,32,768]{3,2,0,1:T(8,128)(2,1)}), bf16[2,8,32,768]{3,2,0,1:T(8,128)(2,1)S(1)}, u32[]{:S(2)}, u32[]{:S(2)}) %all-to-all-start.1) | async-done | bytes 786464 | tf_op jit(solution)/shard_map/all_to_all | solution.py:104
  52.3 2.5 %gather_fusion.5 = bf16[16,128,768]{2,1,0:T(8,128)(2,1)} fusion(bf16[2,128,768]{2,1,0:T(8,128)(2,1)S(1)} %bitcast.125, s32[1024]{0:T(1024)S(1)} %pad_clamp_fusion.2), kind=kCustom, calls=%fused_computation.4.clone | custom fusion | bytes 6291520 | tf_op jit(solution)/shard_map/while/body/eval_jaxpr/jit(_take)/gather | solution.py:30
  57.2 3.9 %gather_fusion.2 = bf16[16,128,768]{2,1,0:T(8,128)(2,1)} fusion(bf16[8,128,768]{2,1,0:T(8,128)(2,1)} %bitcast.122, s32[1024]{0:T(1024)S(1)} %pad_clamp_fusion.6), kind=kCustom, calls=%fused_computation.clone | custom fusion | bytes 6291520 | tf_op jit(solution)/shard_map/while/body/eval_jaxpr/jit(_take)/gather | solution.py:29
  63.6 4.2 %fusion.19 = bf16[16,128,128]{2,1,0:T(8,128)(2,1)S(1)} fusion(bf16[16,128,768]{2,1,0:T(8,128)(2,1)} %gather_fusion.5, pred[16]{0:T(512)(128)(4,1)S(1)} %get-tuple-element.81, bf16[16,128,768]{2,1,0:T(8,128)(2,1)} %gather_fusion.4, pred[16]{0:T(512)(128)(4,1)S(1)} %get-tuple-element.69, pred[16]{0:T(512)(128)(4,1)S(1)} %iota_compare_fusion), kind=kOutput, calls=%fused_computation.45 | convolution fusion | flops 407371776 | bytes 6815792 | tf_op jit(solution)/shard_map/while/body/eval_jaxpr/wzr,wlr->wzl/dot_general | solution.py:31
  67.8 4.2 %fusion.15 = f32[16,128,768]{2,1,0:T(8,128)} fusion(bf16[16,128,128]{2,1,0:T(8,128)(2,1)S(1)} %fusion.19, bf16[16,128,768]{2,1,0:T(8,128)(2,1)S(1)} %copy-done.4, pred[16]{0:T(512)(128)(4,1)S(1)} %get-tuple-element.81), kind=kOutput, calls=%fused_computation.41 | convolution fusion | flops 404226048 | bytes 9961488 | tf_op jit(solution)/shard_map/while/body/eval_jaxpr/nku,nua->nka/dot_general | solution.py:37
  74.4 3.7 %fusion.13 = f32[16,128,768]{2,1,0:T(8,128)} fusion(bf16[16,128,128]{2,1,0:T(8,128)(2,1)S(1)} %fusion.17, bf16[16,128,768]{2,1,0:T(8,128)(2,1)S(1)} %copy-done.3, pred[16]{0:T(512)(128)(4,1)S(1)} %get-tuple-element.85), kind=kOutput, calls=%fused_computation.39 | convolution fusion | flops 404226048 | bytes 9961488 | tf_op jit(solution)/shard_map/while/body/eval_jaxpr/nku,nua->nka/dot_general | solution.py:37
  80.1 15.0 %scatter_fusion.1 = f32[8,128,768]{2,1,0:T(8,128)} fusion(f32[8,128,768]{2,1,0:T(8,128)} %broadcast.485.clone, s32[16]{0:T(128)S(1)} %get-tuple-element.90, f32[16,128,768]{2,1,0:T(8,128)} %fusion.15), kind=kCustom, calls=%fused_computation.9 | custom fusion | flops 1572864 | bytes 18874432 | tf_op jit(solution)/shard_map/while/body/eval_jaxpr/scatter-add | solution.py:43
  95.1 3.9 %broadcast_multiply_fusion = f32[8,128,768]{2,1,0:T(8,128)} fusion(f32[8,128,768]{2,1,0:T(8,128)} %scatter_fusion.1), kind=kLoop, calls=%fused_computation.26 | loop fusion | flops 786432 | bytes 6291456 | tf_op jit(solution)/shard_map/mul | solution.py:58
  100.8 15.2 %scatter_fusion = f32[8,128,768]{2,1,0:T(8,128)} fusion(f32[8,128,768]{2,1,0:T(8,128)} %broadcast.485.clone.1, s32[16]{0:T(128)S(1)} %get-tuple-element.89, f32[16,128,768]{2,1,0:T(8,128)} %fusion.13), kind=kCustom, calls=%fused_computation.8 | custom fusion | flops 1572864 | bytes 18874432 | tf_op jit(solution)/shard_map/while/body/eval_jaxpr/scatter-add | solution.py:43
  124.0 5.8 %fusion.14 = f32[16,128,768]{2,1,0:T(8,128)} fusion(bf16[16,128,128]{2,1,0:T(8,128)(2,1)S(1)} %copy-done.9, bf16[16,128,768]{2,1,0:T(8,128)(2,1)} %gather_fusion.4, pred[16]{0:T(512)(128)(4,1)S(1)} %get-tuple-element.69), kind=kOutput, calls=%fused_computation.40 | convolution fusion | flops 404226048 | bytes 9961488 | tf_op jit(solution)/shard_map/while/body/eval_jaxpr/swc,swj->scj/dot_general | solution.py:40
  129.8 9.2 %scatter_fusion.3 = f32[2,128,768]{2,1,0:T(8,128)S(1)} fusion(f32[2,128,768]{2,1,0:T(8,128)S(1)} %broadcast.493.clone, s32[16]{0:T(128)S(1)} %get-tuple-element.75, f32[16,128,768]{2,1,0:T(8,128)} %fusion.14), kind=kCustom, calls=%fused_computation.11 | custom fusion | flops 1572864 | bytes 18874432 | tf_op jit(solution)/shard_map/while/body/eval_jaxpr/scatter-add | solution.py:46
  139.9 3.7 %all-to-all-start.3 = ((bf16[8,32,768]{2,1,0:T(8,128)(2,1)}), bf16[8,32,768]{2,1,0:T(8,128)(2,1)S(1)}, u32[]{:S(2)}, u32[]{:S(2)}) async-start(bf16[8,32,768]{2,1,0:T(8,128)(2,1)} %bitcast.129), calls=%async_computation.4 | async-start | bytes 786432 | tf_op jit(solution)/shard_map/all_to_all | solution.py:119
  143.6 5.6 %fusion.12 = f32[16,128,768]{2,1,0:T(8,128)} fusion(bf16[16,128,128]{2,1,0:T(8,128)(2,1)S(1)} %copy-done.7, bf16[16,128,768]{2,1,0:T(8,128)(2,1)} %gather_fusion.2, pred[16]{0:T(512)(128)(4,1)S(1)} %get-tuple-element.87), kind=kOutput, calls=%fused_computation.38 | convolution fusion | flops 404226048 | bytes 9961488 | tf_op jit(solution)/shard_map/while/body/eval_jaxpr/swc,swj->scj/dot_general | solution.py:40
  149.2 9.1 %scatter_fusion.2 = f32[2,128,768]{2,1,0:T(8,128)S(1)} fusion(f32[2,128,768]{2,1,0:T(8,128)S(1)} %broadcast.493.clone.1, s32[16]{0:T(128)S(1)} %get-tuple-element.49, f32[16,128,768]{2,1,0:T(8,128)} %fusion.12), kind=kCustom, calls=%fused_computation.10 | custom fusion | flops 1572864 | bytes 18874432 | tf_op jit(solution)/shard_map/while/body/eval_jaxpr/scatter-add | solution.py:46
  159.1 6.1 %all-to-all-start.2 = ((bf16[8,32,768]{2,1,0:T(8,128)(2,1)}), bf16[8,32,768]{2,1,0:T(8,128)(2,1)S(1)}, u32[]{:S(2)}, u32[]{:S(2)}) async-start(bf16[8,32,768]{2,1,0:T(8,128)(2,1)} %bitcast.22), calls=%async_computation.3 | async-start | bytes 786432 | tf_op jit(solution)/shard_map/all_to_all | solution.py:119
  165.9 10.8 %all-to-all-done.2 = bf16[8,32,768]{2,1,0:T(8,128)(2,1)S(1)} async-done(((bf16[8,32,768]{2,1,0:T(8,128)(2,1)}), bf16[8,32,768]{2,1,0:T(8,128)(2,1)S(1)}, u32[]{:S(2)}, u32[]{:S(2)}) %all-to-all-start.2) | async-done | bytes 393248 | tf_op jit(solution)/shard_map/all_to_all | solution.py:119
  178.4 3.6 %all-to-all-start.4 = ((f32[8,32,768]{2,1,0:T(8,128)}), f32[8,32,768]{2,1,0:T(8,128)S(1)}, u32[]{:S(2)}, u32[]{:S(2)}) async-start(f32[8,32,768]{2,1,0:T(8,128)} %convert_add_fusion), calls=%async_computation.5 | async-start | bytes 1572864 | tf_op jit(solution)/shard_map/all_to_all | solution.py:121
  182.0 7.9 %scatter_custom_fusion.4 = f32[256,768]{1,0:T(8,128)S(1)} fusion(s32[1024]{0:T(1024)S(1)} %bitcast.132, bf16[1,1024,768]{2,1,0:T(8,128)(2,1)S(1)} %copy-done.1, f32[1024]{0:T(1024)S(1)} %get-tuple-element.54, f32[]{:T(128)} %constant.153.clone.1), kind=kCustom, calls=%fused_computation.16 | custom fusion | flops 2359296 | bytes 2363396 | tf_op jit(solution)/shard_map/scatter-add | solution.py:72
  190.0 11.7 %all-to-all-done.4 = f32[8,32,768]{2,1,0:T(8,128)S(1)} async-done(((f32[8,32,768]{2,1,0:T(8,128)}), f32[8,32,768]{2,1,0:T(8,128)S(1)}, u32[]{:S(2)}, u32[]{:S(2)}) %all-to-all-start.4) | async-done | bytes 786464 | tf_op jit(solution)/shard_map/all_to_all | solution.py:121
  (77 shorter events, 31.2 us)
Async XLA Ops:
  7.2 50.0 %all-gather.2.cloned.1.call-start = ((), (), s32[]{:S(2)}) async-start(), calls=%async_computation.6 | async-start | bytes 1966080 | tf_op jit(solution)/shard_map/all_gather | solution.py:88
  7.9 19.0 %all-to-all-start = ((bf16[8,32,768]{2,1,0:T(8,128)(2,1)}), bf16[8,32,768]{2,1,0:T(8,128)(2,1)S(1)}, u32[]{:S(2)}, u32[]{:S(2)}) async-start(bf16[8,32,768]{2,1,0:T(8,128)(2,1)} %bitcast.120), calls=%async_computation | async-start | bytes 786432 | tf_op jit(solution)/shard_map/all_to_all | solution.py:97
  23.8 9.0 %copy-start = (bf16[1,256,768]{2,1,0:T(8,128)(2,1)S(1)}, bf16[1,256,768]{2,1,0:T(8,128)(2,1)}, u32[]{:S(2)}) copy-start(bf16[1,256,768]{2,1,0:T(8,128)(2,1)} %param.13) | copy-start | bytes 1179652
  28.5 23.7 %all-to-all-start.1 = ((bf16[2,8,32,768]{3,2,0,1:T(8,128)(2,1)}), bf16[2,8,32,768]{3,2,0,1:T(8,128)(2,1)S(1)}, u32[]{:S(2)}, u32[]{:S(2)}) async-start(bf16[2,8,32,768]{3,2,0,1:T(8,128)(2,1)} %copy.20), calls=%async_computation.1 | async-start | bytes 1572864 | tf_op jit(solution)/shard_map/all_to_all | solution.py:104
  32.2 170.5 %reduce-scatter.2.cloned.1.call-start = ((), (), s32[]{:S(2)}) async-start(), calls=%async_computation.7 | async-start | bytes 3932160 | tf_op jit(solution)/shard_map/reduce_scatter | solution.py:123
  57.2 3.9 %copy-start.1 = (bf16[1,1024,768]{2,1,0:T(8,128)(2,1)S(1)}, bf16[1,1024,768]{2,1,0:T(8,128)(2,1)}, u32[]{:S(2)}) copy-start(bf16[1,1024,768]{2,1,0:T(8,128)(2,1)} %all-gather.2.cloned.1.call-done) | copy-start | bytes 4718596
  63.6 4.3 %copy-start.4 = (bf16[16,128,768]{2,1,0:T(8,128)(2,1)S(1)}, bf16[16,128,768]{2,1,0:T(8,128)(2,1)}, u32[]{:S(2)}) copy-start(bf16[16,128,768]{2,1,0:T(8,128)(2,1)} %gather_fusion.5) | copy-start | bytes 9437188
  67.8 4.3 %copy-start.8 = (bf16[16,128,128]{2,1,0:T(8,128)(2,1)}, bf16[16,128,128]{2,1,0:T(8,128)(2,1)S(1)}, u32[]{:S(2)}) copy-start(bf16[16,128,128]{2,1,0:T(8,128)(2,1)S(1)} %fusion.19) | copy-start | bytes 1572868
  67.8 4.3 %copy-start.2 = (bf16[16,128,768]{2,1,0:T(8,128)(2,1)S(1)}, bf16[16,128,768]{2,1,0:T(8,128)(2,1)}, u32[]{:S(2)}) copy-start(bf16[16,128,768]{2,1,0:T(8,128)(2,1)} %gather_fusion.2) | copy-start | bytes 9437188
  67.8 5.3 %copy-start.3 = (bf16[16,128,768]{2,1,0:T(8,128)(2,1)S(1)}, bf16[16,128,768]{2,1,0:T(8,128)(2,1)}, u32[]{:S(2)}) copy-start(bf16[16,128,768]{2,1,0:T(8,128)(2,1)} %gather_fusion.3) | copy-start | bytes 9437188
  74.4 3.7 %copy-start.6 = (bf16[16,128,128]{2,1,0:T(8,128)(2,1)}, bf16[16,128,128]{2,1,0:T(8,128)(2,1)S(1)}, u32[]{:S(2)}) copy-start(bf16[16,128,128]{2,1,0:T(8,128)(2,1)S(1)} %fusion.17) | copy-start | bytes 1572868
  118.3 1.9 copy-start.5
  122.4 0.7 copy-start.10
  122.4 1.6 copy-start.9
  129.8 13.7 %copy-start.7 = (bf16[16,128,128]{2,1,0:T(8,128)(2,1)S(1)}, bf16[16,128,128]{2,1,0:T(8,128)(2,1)}, u32[]{:S(2)}) copy-start(bf16[16,128,128]{2,1,0:T(8,128)(2,1)} %copy-done.6) | copy-start | bytes 1572868
  139.9 19.3 %all-to-all-start.3 = ((bf16[8,32,768]{2,1,0:T(8,128)(2,1)}), bf16[8,32,768]{2,1,0:T(8,128)(2,1)S(1)}, u32[]{:S(2)}, u32[]{:S(2)}) async-start(bf16[8,32,768]{2,1,0:T(8,128)(2,1)} %bitcast.129), calls=%async_computation.4 | async-start | bytes 786432 | tf_op jit(solution)/shard_map/all_to_all | solution.py:119
  159.1 17.6 %all-to-all-start.2 = ((bf16[8,32,768]{2,1,0:T(8,128)(2,1)}), bf16[8,32,768]{2,1,0:T(8,128)(2,1)S(1)}, u32[]{:S(2)}, u32[]{:S(2)}) async-start(bf16[8,32,768]{2,1,0:T(8,128)(2,1)} %bitcast.22), calls=%async_computation.3 | async-start | bytes 786432 | tf_op jit(solution)/shard_map/all_to_all | solution.py:119
  178.4 23.3 %all-to-all-start.4 = ((f32[8,32,768]{2,1,0:T(8,128)}), f32[8,32,768]{2,1,0:T(8,128)S(1)}, u32[]{:S(2)}, u32[]{:S(2)}) async-start(f32[8,32,768]{2,1,0:T(8,128)} %convert_add_fusion), calls=%async_computation.5 | async-start | bytes 1572864 | tf_op jit(solution)/shard_map/all_to_all | solution.py:121
Sparse Core Ops, SparseCore 0:
  9.6 22.3 all-gather.1
  122.5 36.7 reduce-scatter.1
where the time goes:
time: 210 us
  other arithmetic  73.7 us (35%)
  waiting for transfers between devices  40.8 us (19%)
  local copies, waits for them, and re-layouts  26.2 us (12%)
  matrix products  24.8 us (12%)
  starting transfers between devices  24.4 us (12%)
  between operations  14.4 us (7%)
  blocking collectives  5.27 us (3%)
    scatter-add x2, other arithmetic, one_group(): jax.ops.segment_sum(query_portion, query_index, num_segments=query_tiles)  30.2 us
    scatter-add x2, other arithmetic, one_group(): jax.ops.segment_sum(panel_portion, panel_index, num_segments=panel_tiles)  18.4 us
    all_to_all x1, waiting for transfers between devices, shards(): lax.all_to_all(jnp.take(spread, partner, axis=0), 'idx', split_axis=1, co...  14.5 us
    all_to_all x1, waiting for transfers between devices, shards(): lax.all_to_all(returned, 'idx', split_axis=0, concat_axis=0, tiled=True)  11.7 us
    dot_general x2, matrix products, one_group(): jnp.einsum('swc,swj->scj', sample_weights, query_block_list, preferred_el...  11.3 us
    all_to_all x2, waiting for transfers between devices, shards(): lax.all_to_all(outgoing, 'idx', split_axis=0, concat_axis=0, tiled=True)  10.8 us
    all_to_all x2, starting transfers between devices, shards(): lax.all_to_all(outgoing, 'idx', split_axis=0, concat_axis=0, tiled=True)  9.76 us
    dot_general x2, matrix products, one_group(): jnp.einsum('nku,nua->nka', sample_weights, panel_block_list, preferred_el...  7.94 us
  transfers between devices with their start and end apart: 7, of which 4 were waited for; matrix products, arithmetic and copies ran while one was open for 28% of the time, Pallas kernels for 0%

commit v1 on v0

--- a/solution.py
+++ b/solution.py
@@ -1,8 +1,11 @@
+import functools
 import math
 
 import jax
 import jax.numpy as jnp
 from jax import lax
+from jax.experimental import pallas as pl
+from jax.experimental.pallas import tpu as pltpu
 from jax.sharding import PartitionSpec as P
 
 BLK = 128
@@ -75,7 +78,7 @@
     return (query_near, panel_near)
 
 
-def shards(queries, passages, partner, pair_codes, pair_count, positive):
+def plain_shards(queries, passages, partner, pair_codes, pair_count, positive):
     idx_total = lax.axis_size("idx")
     own_index = lax.axis_index("idx")
     member = lax.axis_index("grp")
@@ -124,6 +127,270 @@
     return (query_total, passage_total[None])
 
 
+def dot_nt(a, b):
+    return lax.dot_general(a, b, (((1,), (1,)), ((), ())), preferred_element_type=jnp.float32)
+
+
+def dot_nn(a, b):
+    return lax.dot_general(a, b, (((1,), (0,)), ((), ())), preferred_element_type=jnp.float32)
+
+
+def dot_tn(a, b):
+    return lax.dot_general(a, b, (((0,), (0,)), ((), ())), preferred_element_type=jnp.float32)
+
+
+def fused_kernel(
+    n, m, rounds, scale,
+    partner_ref, codes_ref, count_ref, q_ref, p_ref, pos_ref,
+    qg_ref, pg_ref,
+    qall, posall, spread, stage, routed, grads, arrived, fin_out, fin_in,
+    part_out, part_in, facc, pacc, wbuf, live,
+    spread_send, spread_recv, q_send, q_recv, pos_send, pos_recv,
+    route_send, route_recv, back_send, back_recv, fin_send, fin_recv, part_send, part_recv,
+):
+    me = lax.axis_index("idx")
+    mg = lax.axis_index("grp")
+    rows, columns = q_ref.shape
+    panel_rows = p_ref.shape[0] * p_ref.shape[1]
+    slots = codes_ref.shape[2]
+    query_blocks, panel_blocks = m * rows // BLK, panel_rows // BLK
+    per_rows = rows // BLK
+
+    barrier = pltpu.get_barrier_semaphore()
+    for d in range(1, n):
+        pl.semaphore_signal(
+            barrier, inc=1, device_id={"idx": lax.rem(me + d, n)}, device_id_type=pl.DeviceIdType.MESH
+        )
+    for d in range(1, m):
+        pl.semaphore_signal(
+            barrier, inc=1, device_id={"grp": lax.rem(mg + d, m)}, device_id_type=pl.DeviceIdType.MESH
+        )
+    pl.semaphore_wait(barrier, n + m - 2)
+
+    def idx_copy(src, dst, send, recv, d):
+        return pltpu.make_async_remote_copy(
+            src_ref=src, dst_ref=dst, send_sem=send, recv_sem=recv,
+            device_id={"idx": lax.rem(me + d, n)}, device_id_type=pl.DeviceIdType.MESH,
+        )
+
+    def grp_copy(src, dst, send, recv, d):
+        return pltpu.make_async_remote_copy(
+            src_ref=src, dst_ref=dst, send_sem=send, recv_sem=recv,
+            device_id={"grp": lax.rem(mg + d, m)}, device_id_type=pl.DeviceIdType.MESH,
+        )
+
+    def spread_copy(d):
+        return idx_copy(p_ref.at[lax.rem(me + d, n)], spread.at[me], spread_send.at[d], spread_recv.at[d], d)
+
+    def route_copy(r, d):
+        return idx_copy(
+            stage.at[r, lax.rem(me + d, n)], routed.at[r, me], route_send.at[r, d], route_recv.at[r, d], d
+        )
+
+    def back_copy(r, d):
+        return idx_copy(
+            grads.at[r, lax.rem(me + d, n)], arrived.at[r, me], back_send.at[r, d], back_recv.at[r, d], d
+        )
+
+    def fin_copy(d):
+        return idx_copy(fin_out.at[lax.rem(me + d, n)], fin_in.at[me], fin_send.at[d], fin_recv.at[d], d)
+
+    def q_copy(d):
+        return grp_copy(q_ref, qall.at[mg], q_send.at[d], q_recv.at[d], d)
+
+    def pos_copy(d):
+        return grp_copy(pos_ref, posall.at[mg], pos_send.at[d], pos_recv.at[d], d)
+
+    def part_copy(d):
+        return grp_copy(
+            part_out.at[lax.rem(mg + d, m)], part_in.at[mg], part_send.at[d], part_recv.at[d], d
+        )
+
+    for d in range(1, n):
+        spread_copy(d).start()
+    for d in range(1, m):
+        pos_copy(d).start()
+        q_copy(d).start()
+    spread[me] = p_ref[me]
+    qall[mg] = q_ref[...]
+    posall[mg] = pos_ref[...]
+
+    code_at = panel_blocks * lax.broadcasted_iota(jnp.int32, (query_blocks, panel_rows), 0) + (
+        lax.broadcasted_iota(jnp.int32, (query_blocks, panel_rows), 1) // BLK
+    )
+    for r in range(rounds):
+        count = count_ref[r, me]
+        hit = jnp.zeros((query_blocks, panel_rows), jnp.float32)
+        for k in range(slots):
+            code = jnp.where(k < count, codes_ref[r, me, k], -1)
+            hit = jnp.where(code_at == code, 1.0, hit)
+        for block in range(query_blocks):
+            live[r, block // per_rows, block % per_rows] = hit[block : block + 1]
+
+    for d in range(1, n):
+        spread_copy(d).wait_recv()
+    for r in range(rounds):
+        for c in range(n):
+            stage[r, c] = spread[partner_ref[r, c]]
+        for d in range(1, n):
+            route_copy(r, d).start()
+        routed[r, me] = stage[r, me]
+
+    for d in range(1, m):
+        pos_copy(d).wait_recv()
+        q_copy(d).wait_recv()
+
+    own = p_ref[...].reshape(panel_rows, columns)
+    panel_row = lax.broadcasted_iota(jnp.int32, (panel_rows, rows), 0) + mg * panel_rows
+    pg_ref[...] = jnp.zeros(pg_ref.shape, jnp.float32)
+
+    def near_block(h, carry):
+        q = qall[h]
+        hit = panel_row == posall[h]
+        score = scale * jnp.sum(jnp.where(hit, dot_nt(own, q), 0.0), axis=0, keepdims=True)
+        coef = positive_weight * (jax.nn.sigmoid(score) - 1.0)
+        weight = jnp.where(hit, coef, 0.0)
+        high = weight.astype(jnp.bfloat16)
+        low = (weight - high.astype(jnp.float32)).astype(jnp.bfloat16)
+        pg_ref[...] += dot_nn(high, q) + dot_nn(low, q)
+        facc[h] = dot_tn(high, own) + dot_tn(low, own)
+        return carry
+
+    lax.fori_loop(0, m, near_block, 0)
+
+    for r in range(rounds):
+        for d in range(1, n):
+            route_copy(r, d).wait_recv()
+        panel = routed[r].reshape(panel_rows, columns)
+        pacc[...] = jnp.zeros(pacc.shape, jnp.float32)
+
+        def score_block(h, carry):
+            q = qall[h]
+            scores = scale * dot_nt(q, panel)
+            mask = jnp.concatenate(
+                [jnp.broadcast_to(live[r, h, b], (BLK, panel_rows)) for b in range(per_rows)], axis=0
+            )
+            weight = jnp.where(mask > 0.0, jax.nn.sigmoid(scores), 0.0).astype(jnp.bfloat16)
+            wbuf[h] = weight
+            pacc[...] += dot_tn(weight, q)
+            return carry
+
+        lax.fori_loop(0, m, score_block, 0)
+        grads[r] = (scale * pacc[...]).astype(jnp.bfloat16).reshape(grads.shape[1:])
+        for d in range(1, n):
+            back_copy(r, d).start()
+        arrived[r, me] = grads[r, me]
+
+        if r < rounds - 1:
+            def query_block(h, carry):
+                facc[h] += dot_nn(wbuf[h], panel)
+                return carry
+
+            lax.fori_loop(0, m, query_block, 0)
+        else:
+            def last_block(d, carry):
+                h = lax.rem(mg + d, m)
+                part_out[h] = (scale * (facc[h] + dot_nn(wbuf[h], panel))).astype(jnp.bfloat16)
+                part_copy(d).start()
+                return carry
+
+            lax.fori_loop(1, m, last_block, 0)
+            qg_ref[...] = scale * (facc[mg] + dot_nn(wbuf[mg], panel))
+
+    for r in range(rounds):
+        for d in range(1, n):
+            back_copy(r, d).wait_recv()
+    for j in range(n):
+        total = jnp.zeros(fin_out.shape[1:], jnp.float32)
+        for r in range(rounds):
+            source = jnp.int32(0)
+            for c in range(n):
+                source = jnp.where(partner_ref[r, c] == j, c, source)
+            total = total + arrived[r, source].astype(jnp.float32)
+        fin_out[j] = total.astype(jnp.bfloat16)
+    for d in range(1, n):
+        fin_copy(d).start()
+    fin_in[me] = fin_out[me]
+
+    for d in range(1, m):
+        part_copy(d).wait_recv()
+        qg_ref[...] += part_in[lax.rem(mg + m - d, m)].astype(jnp.float32)
+
+    for d in range(1, n):
+        fin_copy(d).wait_recv()
+    pg_ref[...] = scale * pg_ref[...] + fin_in[...].reshape(panel_rows, columns).astype(jnp.float32)
+
+    for d in range(1, n):
+        spread_copy(d).wait_send()
+        fin_copy(d).wait_send()
+        for r in range(rounds):
+            route_copy(r, d).wait_send()
+            back_copy(r, d).wait_send()
+    for d in range(1, m):
+        q_copy(d).wait_send()
+        pos_copy(d).wait_send()
+        part_copy(d).wait_send()
+
+
+def fused_shards(queries, passages, partner, pair_codes, pair_count, positive):
+    n, m = lax.axis_size("idx"), lax.axis_size("grp")
+    rounds = partner.shape[0]
+    rows, columns = queries.shape[1:]
+    panel_rows = passages.shape[1]
+    piece = panel_rows // n
+    slots = pair_codes.shape[3]
+    bf16, f32, dma = jnp.bfloat16, jnp.float32, pltpu.SemaphoreType.DMA
+    vmem, smem = pl.BlockSpec(memory_space=pltpu.VMEM), pl.BlockSpec(memory_space=pltpu.SMEM)
+    pieces = (n, piece, columns)
+    query_grad, passage_grad = pl.pallas_call(
+        functools.partial(fused_kernel, n, m, rounds, columns ** (-0.5)),
+        out_shape=(
+            jax.ShapeDtypeStruct((rows, columns), f32),
+            jax.ShapeDtypeStruct((panel_rows, columns), f32),
+        ),
+        in_specs=[smem] * 3 + [vmem] * 3,
+        out_specs=(vmem, vmem),
+        scratch_shapes=[
+            pltpu.VMEM((m, rows, columns), bf16),
+            pltpu.VMEM((m, 1, rows), jnp.int32),
+            pltpu.VMEM(pieces, bf16),
+            pltpu.VMEM((rounds,) + pieces, bf16),
+            pltpu.VMEM((rounds,) + pieces, bf16),
+            pltpu.VMEM((rounds,) + pieces, bf16),
+            pltpu.VMEM((rounds,) + pieces, bf16),
+            pltpu.VMEM(pieces, bf16),
+            pltpu.VMEM(pieces, bf16),
+            pltpu.VMEM((m, rows, columns), bf16),
+            pltpu.VMEM((m, rows, columns), bf16),
+            pltpu.VMEM((m, rows, columns), f32),
+            pltpu.VMEM((panel_rows, columns), f32),
+            pltpu.VMEM((m, rows, panel_rows), bf16),
+            pltpu.VMEM((rounds, m, rows // BLK, 1, panel_rows), f32),
+            dma((n,)), dma((n,)), dma((m,)), dma((m,)), dma((m,)), dma((m,)),
+            dma((rounds, n)), dma((rounds, n)), dma((rounds, n)), dma((rounds, n)),
+            dma((n,)), dma((n,)), dma((m,)), dma((m,)),
+        ],
+        compiler_params=pltpu.CompilerParams(
+            collective_id=0, has_side_effects=True, vmem_limit_bytes=40 * 1024 * 1024
+        ),
+    )(
+        partner,
+        pair_codes.reshape(rounds, n, slots),
+        pair_count.reshape(rounds, n),
+        queries[0],
+        passages.reshape(pieces),
+        positive,
+    )
+    return (query_grad[None], passage_grad[None])
+
+
+def shards(queries, passages, partner, pair_codes, pair_count, positive):
+    n = lax.axis_size("idx")
+    if passages.shape[1] % (16 * n) == 0 and partner.shape[1] == n:
+        return fused_shards(queries, passages, partner, pair_codes, pair_count, positive)
+    return plain_shards(queries, passages, partner, pair_codes, pair_count, positive)
+
+
 def solution(mesh):
     in_specs = (
         P("idx", "grp", None),

time: 210 us -> 70.4 us (0.34)
  the two profiles are of different devices: /device:TPU:0 before, /device:TPU:20 now
where the time goes in v1:
time: 70.4 us; the launch traced here: 70.1 us
  Pallas kernels  64.3 us (91%)
  local copies, waits for them, and re-layouts  5.13 us (7%)
    pallas_call x1, Pallas kernels, fused_shards(): pl.pallas_call(functools.partial(fused_kernel, n, m, rounds, columns ** (...  64.3 us
    unnamed x14, local copies, waits for them, and re-layouts  5.13 us

profile of v1, /device:TPU:20, one launch (start us, length us, event | category | flops | bytes accessed | tf_op | source)
XLA Modules:
  0.0 70.1 jit_solution(2223846326187673645)
XLA Ops:
  0.6 0.0 copy-start.4
  0.6 0.0 copy-start.5
  0.7 0.0 copy-start.3
  0.7 0.7 copy-done.4
  1.3 0.0 copy-done.5
  1.3 0.0 copy-done.3
  1.3 0.0 copy-start
  1.3 1.0 %copy-done = bf16[1,256,768]{2,1,0:T(8,128)(2,1)S(1)} copy-done((bf16[1,256,768]{2,1,0:T(8,128)(2,1)S(1)}, bf16[1,256,768]{2,1,0:T(8,128)(2,1)}, u32[]{:S(2)}) %copy-start) | copy-done | bytes 393240
  2.3 0.0 copy-start.1
  2.3 1.0 %copy-done.1 = bf16[1,256,768]{2,1,0:T(8,128)(2,1)S(1)} copy-done((bf16[1,256,768]{2,1,0:T(8,128)(2,1)S(1)}, bf16[1,256,768]{2,1,0:T(8,128)(2,1)}, u32[]{:S(2)}) %copy-start.1) | copy-done | bytes 393240
  3.3 0.0 copy-start.2
  3.3 0.7 copy-done.2
  4.0 64.3 %shard_map.77 = (f32[256,768]{1,0:T(8,128)S(1)}, f32[256,768]{1,0:T(8,128)S(1)}) custom-call(s32[2,8]{1,0:T(2,128)S(1)} %copy-done.3, s32[2,8,16]{2,1,0:T(8,128)S(1)} %bitcast.10, s32[2,8]{1,0:T(2,128)S(1)} %bitcast.11, bf16[256,768]{1,0:T(8,128)(2,1)S(1)} %bitcast.8, bf16[8,32,768]{2,1,0:T(8,128)(2,1)S(1)} %bitcast.9, s32[1,256]{1,0:T(1,128)S(1)} %copy-done.5), custom_call_target="tpu_custom_call" | custom-call | tf_op jit(solution)/shard_map/pallas_call | solution.py:345
  68.4 0.9 %copy.10 = f32[1,256,768]{2,1,0:T(8,128)} copy(f32[1,256,768]{2,1,0:T(8,128)S(1)} %bitcast.7) | data formatting | bytes 1572864
  69.3 0.9 %copy.11 = f32[1,256,768]{2,1,0:T(8,128)} copy(f32[1,256,768]{2,1,0:T(8,128)S(1)} %bitcast.6) | data formatting | bytes 1572864
Async XLA Ops:
  0.6 0.7 copy-start.4
  0.6 0.7 copy-start.5
  0.7 0.7 copy-start.3
  1.3 1.0 %copy-start = (bf16[1,256,768]{2,1,0:T(8,128)(2,1)S(1)}, bf16[1,256,768]{2,1,0:T(8,128)(2,1)}, u32[]{:S(2)}) copy-start(bf16[1,256,768]{2,1,0:T(8,128)(2,1)} %param.6) | copy-start | bytes 1179652
  2.3 1.0 %copy-start.1 = (bf16[1,256,768]{2,1,0:T(8,128)(2,1)S(1)}, bf16[1,256,768]{2,1,0:T(8,128)(2,1)}, u32[]{:S(2)}) copy-start(bf16[1,256,768]{2,1,0:T(8,128)(2,1)} %param.7) | copy-start | bytes 1179652
  3.3 0.7 copy-start.2

commit v2 on v1

--- a/solution.py
+++ b/solution.py
@@ -144,7 +144,7 @@
     partner_ref, codes_ref, count_ref, q_ref, p_ref, pos_ref,
     qg_ref, pg_ref,
     qall, posall, spread, stage, routed, grads, arrived, fin_out, fin_in,
-    part_out, part_in, facc, pacc, wbuf, live,
+    part_out, part_in, facc, pacc, wbuf, live, own_panel, local_sem,
     spread_send, spread_recv, q_send, q_recv, pos_send, pos_recv,
     route_send, route_recv, back_send, back_recv, fin_send, fin_recv, part_send, part_recv,
 ):
@@ -156,6 +156,14 @@
     query_blocks, panel_blocks = m * rows // BLK, panel_rows // BLK
     per_rows = rows // BLK
 
+    local = [
+        pltpu.make_async_copy(p_ref.at[me], spread.at[me], local_sem.at[0]),
+        pltpu.make_async_copy(q_ref, qall.at[mg], local_sem.at[1]),
+        pltpu.make_async_copy(p_ref, own_panel, local_sem.at[2]),
+    ]
+    for copy in local:
+        copy.start()
+
     barrier = pltpu.get_barrier_semaphore()
     for d in range(1, n):
         pl.semaphore_signal(
@@ -211,8 +219,6 @@
     for d in range(1, m):
         pos_copy(d).start()
         q_copy(d).start()
-    spread[me] = p_ref[me]
-    qall[mg] = q_ref[...]
     posall[mg] = pos_ref[...]
 
     code_at = panel_blocks * lax.broadcasted_iota(jnp.int32, (query_blocks, panel_rows), 0) + (
@@ -227,12 +233,16 @@
         for block in range(query_blocks):
             live[r, block // per_rows, block % per_rows] = hit[block : block + 1]
 
+    for copy in local:
+        copy.wait()
     for d in range(1, n):
         spread_copy(d).wait_recv()
     for r in range(rounds):
         for c in range(n):
             stage[r, c] = spread[partner_ref[r, c]]
         for d in range(1, n):
+            if r > 0:
+                route_copy(r - 1, d).wait_send()
             route_copy(r, d).start()
         routed[r, me] = stage[r, me]
 
@@ -240,7 +250,7 @@
         pos_copy(d).wait_recv()
         q_copy(d).wait_recv()
 
-    own = p_ref[...].reshape(panel_rows, columns)
+    own = own_panel[...].reshape(panel_rows, columns)
     panel_row = lax.broadcasted_iota(jnp.int32, (panel_rows, rows), 0) + mg * panel_rows
     pg_ref[...] = jnp.zeros(pg_ref.shape, jnp.float32)
 
@@ -256,8 +266,6 @@
         facc[h] = dot_tn(high, own) + dot_tn(low, own)
         return carry
 
-    lax.fori_loop(0, m, near_block, 0)
-
     for r in range(rounds):
         for d in range(1, n):
             route_copy(r, d).wait_recv()
@@ -280,6 +288,9 @@
         for d in range(1, n):
             back_copy(r, d).start()
         arrived[r, me] = grads[r, me]
+
+        if r == 0:
+            lax.fori_loop(0, m, near_block, 0)
 
         if r < rounds - 1:
             def query_block(h, carry):
@@ -322,9 +333,9 @@
 
     for d in range(1, n):
         spread_copy(d).wait_send()
+        route_copy(rounds - 1, d).wait_send()
         fin_copy(d).wait_send()
         for r in range(rounds):
-            route_copy(r, d).wait_send()
             back_copy(r, d).wait_send()
     for d in range(1, m):
         q_copy(d).wait_send()
@@ -341,6 +352,7 @@
     slots = pair_codes.shape[3]
     bf16, f32, dma = jnp.bfloat16, jnp.float32, pltpu.SemaphoreType.DMA
     vmem, smem = pl.BlockSpec(memory_space=pltpu.VMEM), pl.BlockSpec(memory_space=pltpu.SMEM)
+    hbm = pl.BlockSpec(memory_space=pl.ANY)
     pieces = (n, piece, columns)
     query_grad, passage_grad = pl.pallas_call(
         functools.partial(fused_kernel, n, m, rounds, columns ** (-0.5)),
@@ -348,7 +360,7 @@
             jax.ShapeDtypeStruct((rows, columns), f32),
             jax.ShapeDtypeStruct((panel_rows, columns), f32),
         ),
-        in_specs=[smem] * 3 + [vmem] * 3,
+        in_specs=[smem] * 3 + [hbm] * 2 + [vmem],
         out_specs=(vmem, vmem),
         scratch_shapes=[
             pltpu.VMEM((m, rows, columns), bf16),
@@ -366,12 +378,14 @@
             pltpu.VMEM((panel_rows, columns), f32),
             pltpu.VMEM((m, rows, panel_rows), bf16),
             pltpu.VMEM((rounds, m, rows // BLK, 1, panel_rows), f32),
+            pltpu.VMEM(pieces, bf16),
+            dma((3,)),
             dma((n,)), dma((n,)), dma((m,)), dma((m,)), dma((m,)), dma((m,)),
             dma((rounds, n)), dma((rounds, n)), dma((rounds, n)), dma((rounds, n)),
             dma((n,)), dma((n,)), dma((m,)), dma((m,)),
         ],
         compiler_params=pltpu.CompilerParams(
-            collective_id=0, has_side_effects=True, vmem_limit_bytes=40 * 1024 * 1024
+            collective_id=0, has_side_effects=True, vmem_limit_bytes=56 * 1024 * 1024
         ),
     )(
         partner,

time: 70.4 us -> 68.1 us (0.967)
  the two profiles are of different devices: /device:TPU:20 before, /device:TPU:0 now
where the time goes in v2:
time: 68.1 us; the launch traced here: 67.9 us
  Pallas kernels  64.2 us (94%)
  local copies, waits for them, and re-layouts  3.02 us (4%)
    pallas_call x1, Pallas kernels, fused_shards(): pl.pallas_call(functools.partial(fused_kernel, n, m, rounds, columns ** (...  64.2 us
    unnamed x4, local copies, waits for them, and re-layouts  3.02 us

profile of v2, /device:TPU:0, one launch (start us, length us, event | category | flops | bytes accessed | tf_op | source)
XLA Modules:
  0.0 67.9 jit_solution(5514100349933057553)
XLA Ops:
  0.6 64.2 %shard_map.77 = (f32[256,768]{1,0:T(8,128)}, f32[256,768]{1,0:T(8,128)}) custom-call(s32[2,8]{1,0:T(2,128)} %partner_ref.1, s32[2,8,16]{2,1,0:T(8,128)} %bitcast.10, s32[2,8]{1,0:T(2,128)} %bitcast.11, bf16[256,768]{1,0:T(8,128)(2,1)} %bitcast.8, bf16[8,32,768]{2,1,0:T(8,128)(2,1)} %bitcast.9, s32[1,256]{1,0:T(1,128)} %pos_ref.1), custom_call_target="tpu_custom_call" | custom-call | tf_op jit(solution)/shard_map/pallas_call | solution.py:357
  64.9 0.0 copy-start
  64.9 2.1 %copy.10 = f32[1,256,768]{2,1,0:T(8,128)} copy(f32[1,256,768]{2,1,0:T(8,128)} %bitcast.7) | data formatting | bytes 1572864
  67.0 0.0 copy-done
  67.0 0.9 %copy.11 = f32[1,256,768]{2,1,0:T(8,128)} copy(f32[1,256,768]{2,1,0:T(8,128)S(1)} %bitcast.6) | data formatting | bytes 1572864
Async XLA Ops:
  64.9 2.1 %copy-start = (f32[256,768]{1,0:T(8,128)S(1)}, f32[256,768]{1,0:T(8,128)}, u32[]{:S(2)}) copy-start(f32[256,768]{1,0:T(8,128)} %get-tuple-element.5) | copy-start | bytes 2359300

commit v3 on v2

--- a/solution.py
+++ b/solution.py
@@ -143,7 +143,7 @@
     n, m, rounds, scale,
     partner_ref, codes_ref, count_ref, q_ref, p_ref, pos_ref,
     qg_ref, pg_ref,
-    qall, posall, spread, stage, routed, grads, arrived, fin_out, fin_in,
+    qall, posall, spread_a, spread_b, stage, routed, grads, arrived, last_a, last_b, fin_out, fin_in,
     part_out, part_in, facc, pacc, wbuf, live, own_panel, local_sem,
     spread_send, spread_recv, q_send, q_recv, pos_send, pos_recv,
     route_send, route_recv, back_send, back_recv, fin_send, fin_recv, part_send, part_recv,
@@ -155,11 +155,28 @@
     slots = codes_ref.shape[2]
     query_blocks, panel_blocks = m * rows // BLK, panel_rows // BLK
     per_rows = rows // BLK
+    piece = p_ref.shape[1]
+    spread, last = (spread_a, spread_b), (last_a, last_b)
+    chunks = len(spread)
+    steps = sorted(range(1, n), key=lambda d: -min(d, n - d))
+
+    def route_parts(r):
+        return chunks if r == 0 else 1
+
+    def back_parts(r):
+        return chunks if r == rounds - 1 else 1
+
+    def part_rows(h, parts):
+        return pl.ds(h * (piece // parts), piece // parts)
 
     local = [
-        pltpu.make_async_copy(p_ref.at[me], spread.at[me], local_sem.at[0]),
-        pltpu.make_async_copy(q_ref, qall.at[mg], local_sem.at[1]),
-        pltpu.make_async_copy(p_ref, own_panel, local_sem.at[2]),
+        pltpu.make_async_copy(q_ref, qall.at[mg], local_sem.at[0]),
+        pltpu.make_async_copy(p_ref, own_panel, local_sem.at[1]),
+    ] + [
+        pltpu.make_async_copy(
+            p_ref.at[me, part_rows(h, chunks)], spread[h].at[me], local_sem.at[2 + h]
+        )
+        for h in range(chunks)
     ]
     for copy in local:
         copy.start()
@@ -187,21 +204,34 @@
             device_id={"grp": lax.rem(mg + d, m)}, device_id_type=pl.DeviceIdType.MESH,
         )
 
-    def spread_copy(d):
-        return idx_copy(p_ref.at[lax.rem(me + d, n)], spread.at[me], spread_send.at[d], spread_recv.at[d], d)
-
-    def route_copy(r, d):
+    def spread_copy(h, d):
+        span = part_rows(h, chunks)
         return idx_copy(
-            stage.at[r, lax.rem(me + d, n)], routed.at[r, me], route_send.at[r, d], route_recv.at[r, d], d
-        )
-
-    def back_copy(r, d):
+            p_ref.at[lax.rem(me + d, n), span], spread[h].at[me],
+            spread_send.at[h, d], spread_recv.at[h, d], d,
+        )
+
+    def route_copy(r, h, d):
+        span = part_rows(h, route_parts(r))
         return idx_copy(
-            grads.at[r, lax.rem(me + d, n)], arrived.at[r, me], back_send.at[r, d], back_recv.at[r, d], d
-        )
-
-    def fin_copy(d):
-        return idx_copy(fin_out.at[lax.rem(me + d, n)], fin_in.at[me], fin_send.at[d], fin_recv.at[d], d)
+            stage.at[r, lax.rem(me + d, n), span], routed.at[r, me, span],
+            route_send.at[r, h, d], route_recv.at[r, h, d], d,
+        )
+
+    def back_copy(r, h, d):
+        span = part_rows(h, back_parts(r))
+        return idx_copy(
+            grads.at[r, lax.rem(me + d, n), span],
+            last[h].at[me] if r == rounds - 1 else arrived.at[r, me],
+            back_send.at[r, h, d], back_recv.at[r, h, d], d,
+        )
+
+    def fin_copy(h, d):
+        span = part_rows(h, chunks)
+        return idx_copy(
+            fin_out.at[lax.rem(me + d, n), span], fin_in.at[me, span],
+            fin_send.at[h, d], fin_recv.at[h, d], d,
+        )
 
     def q_copy(d):
         return grp_copy(q_ref, qall.at[mg], q_send.at[d], q_recv.at[d], d)
@@ -214,8 +244,9 @@
             part_out.at[lax.rem(mg + d, m)], part_in.at[mg], part_send.at[d], part_recv.at[d], d
         )
 
-    for d in range(1, n):
-        spread_copy(d).start()
+    for h in range(chunks):
+        for d in steps:
+            spread_copy(h, d).start()
     for d in range(1, m):
         pos_copy(d).start()
         q_copy(d).start()
@@ -235,15 +266,23 @@
 
     for copy in local:
         copy.wait()
-    for d in range(1, n):
-        spread_copy(d).wait_recv()
-    for r in range(rounds):
+    for h in range(chunks):
+        span = part_rows(h, chunks)
+        for d in steps:
+            spread_copy(h, d).wait_recv()
         for c in range(n):
-            stage[r, c] = spread[partner_ref[r, c]]
-        for d in range(1, n):
-            if r > 0:
-                route_copy(r - 1, d).wait_send()
-            route_copy(r, d).start()
+            stage[0, c, span] = spread[h][partner_ref[0, c]]
+        for d in steps:
+            route_copy(0, h, d).start()
+    routed[0, me] = stage[0, me]
+    for r in range(1, rounds):
+        for c in range(n):
+            for h in range(chunks):
+                stage[r, c, part_rows(h, chunks)] = spread[h][partner_ref[r, c]]
+        for d in steps:
+            for h in range(route_parts(r - 1)):
+                route_copy(r - 1, h, d).wait_send()
+            route_copy(r, 0, d).start()
         routed[r, me] = stage[r, me]
 
     for d in range(1, m):
@@ -267,8 +306,9 @@
         return carry
 
     for r in range(rounds):
-        for d in range(1, n):
-            route_copy(r, d).wait_recv()
+        for h in range(route_parts(r)):
+            for d in steps:
+                route_copy(r, h, d).wait_recv()
         panel = routed[r].reshape(panel_rows, columns)
         pacc[...] = jnp.zeros(pacc.shape, jnp.float32)
 
@@ -285,9 +325,14 @@
 
         lax.fori_loop(0, m, score_block, 0)
         grads[r] = (scale * pacc[...]).astype(jnp.bfloat16).reshape(grads.shape[1:])
-        for d in range(1, n):
-            back_copy(r, d).start()
-        arrived[r, me] = grads[r, me]
+        for h in range(back_parts(r)):
+            for d in steps:
+                back_copy(r, h, d).start()
+        if r < rounds - 1:
+            arrived[r, me] = grads[r, me]
+        else:
+            for h in range(chunks):
+                last[h][me] = grads[r, me, part_rows(h, chunks)]
 
         if r == 0:
             lax.fori_loop(0, m, near_block, 0)
@@ -308,35 +353,47 @@
             lax.fori_loop(1, m, last_block, 0)
             qg_ref[...] = scale * (facc[mg] + dot_nn(wbuf[mg], panel))
 
+    for r in range(rounds - 1):
+        for d in steps:
+            back_copy(r, 0, d).wait_recv()
+    sources = []
     for r in range(rounds):
-        for d in range(1, n):
-            back_copy(r, d).wait_recv()
-    for j in range(n):
-        total = jnp.zeros(fin_out.shape[1:], jnp.float32)
-        for r in range(rounds):
+        for j in range(n):
             source = jnp.int32(0)
             for c in range(n):
                 source = jnp.where(partner_ref[r, c] == j, c, source)
-            total = total + arrived[r, source].astype(jnp.float32)
-        fin_out[j] = total.astype(jnp.bfloat16)
-    for d in range(1, n):
-        fin_copy(d).start()
+            sources.append(source)
+    for h in range(chunks):
+        span = part_rows(h, chunks)
+        for d in steps:
+            back_copy(rounds - 1, h, d).wait_recv()
+        for j in range(n):
+            total = last[h][sources[(rounds - 1) * n + j]].astype(jnp.float32)
+            for r in range(rounds - 1):
+                total = total + arrived[r, sources[r * n + j], span].astype(jnp.float32)
+            fin_out[j, span] = total.astype(jnp.bfloat16)
+        for d in steps:
+            fin_copy(h, d).start()
     fin_in[me] = fin_out[me]
 
     for d in range(1, m):
         part_copy(d).wait_recv()
         qg_ref[...] += part_in[lax.rem(mg + m - d, m)].astype(jnp.float32)
 
-    for d in range(1, n):
-        fin_copy(d).wait_recv()
+    for h in range(chunks):
+        for d in steps:
+            fin_copy(h, d).wait_recv()
     pg_ref[...] = scale * pg_ref[...] + fin_in[...].reshape(panel_rows, columns).astype(jnp.float32)
 
-    for d in range(1, n):
-        spread_copy(d).wait_send()
-        route_copy(rounds - 1, d).wait_send()
-        fin_copy(d).wait_send()
+    for d in steps:
+        for h in range(chunks):
+            spread_copy(h, d).wait_send()
+            fin_copy(h, d).wait_send()
+        for h in range(route_parts(rounds - 1)):
+            route_copy(rounds - 1, h, d).wait_send()
         for r in range(rounds):
-            back_copy(r, d).wait_send()
+            for h in range(back_parts(r)):
+                back_copy(r, h, d).wait_send()
     for d in range(1, m):
         q_copy(d).wait_send()
         pos_copy(d).wait_send()
@@ -353,7 +410,7 @@
     bf16, f32, dma = jnp.bfloat16, jnp.float32, pltpu.SemaphoreType.DMA
     vmem, smem = pl.BlockSpec(memory_space=pltpu.VMEM), pl.BlockSpec(memory_space=pltpu.SMEM)
     hbm = pl.BlockSpec(memory_space=pl.ANY)
-    pieces = (n, piece, columns)
+    pieces, halves = (n, piece, columns), (n, piece // 2, columns)
     query_grad, passage_grad = pl.pallas_call(
         functools.partial(fused_kernel, n, m, rounds, columns ** (-0.5)),
         out_shape=(
@@ -365,11 +422,14 @@
         scratch_shapes=[
             pltpu.VMEM((m, rows, columns), bf16),
             pltpu.VMEM((m, 1, rows), jnp.int32),
-            pltpu.VMEM(pieces, bf16),
+            pltpu.VMEM(halves, bf16),
+            pltpu.VMEM(halves, bf16),
             pltpu.VMEM((rounds,) + pieces, bf16),
             pltpu.VMEM((rounds,) + pieces, bf16),
             pltpu.VMEM((rounds,) + pieces, bf16),
-            pltpu.VMEM((rounds,) + pieces, bf16),
+            pltpu.VMEM((max(rounds - 1, 1),) + pieces, bf16),
+            pltpu.VMEM(halves, bf16),
+            pltpu.VMEM(halves, bf16),
             pltpu.VMEM(pieces, bf16),
             pltpu.VMEM(pieces, bf16),
             pltpu.VMEM((m, rows, columns), bf16),
@@ -379,10 +439,10 @@
             pltpu.VMEM((m, rows, panel_rows), bf16),
             pltpu.VMEM((rounds, m, rows // BLK, 1, panel_rows), f32),
             pltpu.VMEM(pieces, bf16),
-            dma((3,)),
-            dma((n,)), dma((n,)), dma((m,)), dma((m,)), dma((m,)), dma((m,)),
-            dma((rounds, n)), dma((rounds, n)), dma((rounds, n)), dma((rounds, n)),
-            dma((n,)), dma((n,)), dma((m,)), dma((m,)),
+            dma((4,)),
+            dma((2, n)), dma((2, n)), dma((m,)), dma((m,)), dma((m,)), dma((m,)),
+            dma((rounds, 2, n)), dma((rounds, 2, n)), dma((rounds, 2, n)), dma((rounds, 2, n)),
+            dma((2, n)), dma((2, n)), dma((m,)), dma((m,)),
         ],
         compiler_params=pltpu.CompilerParams(
             collective_id=0, has_side_effects=True, vmem_limit_bytes=56 * 1024 * 1024
@@ -400,7 +460,7 @@
 
 def shards(queries, passages, partner, pair_codes, pair_count, positive):
     n = lax.axis_size("idx")
-    if passages.shape[1] % (16 * n) == 0 and partner.shape[1] == n:
+    if passages.shape[1] % (32 * n) == 0 and partner.shape[1] == n:
         return fused_shards(queries, passages, partner, pair_codes, pair_count, positive)
     return plain_shards(queries, passages, partner, pair_codes, pair_count, positive)
 

time: 68.1 us -> 67 us (0.984)
  Pallas kernels: 64.2 us -> 63.1 us
    pallas_call x1, Pallas kernels: 64.2 us -> 63.1 us  [fused_shards(): pl.pallas_call(functools.partial(fused_kernel, n, m, rounds, columns ** (...]
where the time goes in v3:
time: 67 us; the launch traced here: 66.8 us
  Pallas kernels  63.1 us (94%)
  local copies, waits for them, and re-layouts  3.02 us (5%)
    pallas_call x1, Pallas kernels, fused_shards(): pl.pallas_call(functools.partial(fused_kernel, n, m, rounds, columns ** (...  63.1 us
    unnamed x4, local copies, waits for them, and re-layouts  3.02 us

profile of v3, /device:TPU:0, one launch (start us, length us, event | category | flops | bytes accessed | tf_op | source)
XLA Modules:
  0.0 66.8 jit_solution(6224198032426232178)
XLA Ops:
  0.6 63.1 %shard_map.77 = (f32[256,768]{1,0:T(8,128)}, f32[256,768]{1,0:T(8,128)}) custom-call(s32[2,8]{1,0:T(2,128)} %partner_ref.1, s32[2,8,16]{2,1,0:T(8,128)} %bitcast.10, s32[2,8]{1,0:T(2,128)} %bitcast.11, bf16[256,768]{1,0:T(8,128)(2,1)} %bitcast.8, bf16[8,32,768]{2,1,0:T(8,128)(2,1)} %bitcast.9, s32[1,256]{1,0:T(1,128)} %pos_ref.1), custom_call_target="tpu_custom_call" | custom-call | tf_op jit(solution)/shard_map/pallas_call | solution.py:414
  63.7 0.0 copy-start
  63.8 2.1 %copy.10 = f32[1,256,768]{2,1,0:T(8,128)} copy(f32[1,256,768]{2,1,0:T(8,128)} %bitcast.7) | data formatting | bytes 1572864
  65.9 0.0 copy-done
  65.9 0.9 %copy.11 = f32[1,256,768]{2,1,0:T(8,128)} copy(f32[1,256,768]{2,1,0:T(8,128)S(1)} %bitcast.6) | data formatting | bytes 1572864
Async XLA Ops:
  63.7 2.1 %copy-start = (f32[256,768]{1,0:T(8,128)S(1)}, f32[256,768]{1,0:T(8,128)}, u32[]{:S(2)}) copy-start(f32[256,768]{1,0:T(8,128)} %get-tuple-element.5) | copy-start | bytes 2359300

commit v4 on v3

--- a/solution.py
+++ b/solution.py
@@ -233,23 +233,34 @@
             fin_send.at[h, d], fin_recv.at[h, d], d,
         )
 
-    def q_copy(d):
-        return grp_copy(q_ref, qall.at[mg], q_send.at[d], q_recv.at[d], d)
+    sibling = mg + 1 - 2 * lax.rem(mg, 2)
+    across = lax.rem(mg + 2, m)
+
+    def member_copy(src, dst, send, recv, target):
+        return pltpu.make_async_remote_copy(
+            src_ref=src, dst_ref=dst, send_sem=send, recv_sem=recv,
+            device_id={"grp": target}, device_id_type=pl.DeviceIdType.MESH,
+        )
+
+    q_to_across = member_copy(q_ref, qall.at[mg], q_send.at[0], q_recv.at[0], across)
+    q_to_sibling = member_copy(q_ref, qall.at[mg], q_send.at[1], q_recv.at[1], sibling)
+    q_forward = member_copy(qall.at[across], qall.at[across], q_send.at[2], q_recv.at[2], sibling)
 
     def pos_copy(d):
         return grp_copy(pos_ref, posall.at[mg], pos_send.at[d], pos_recv.at[d], d)
 
-    def part_copy(d):
-        return grp_copy(
-            part_out.at[lax.rem(mg + d, m)], part_in.at[mg], part_send.at[d], part_recv.at[d], d
-        )
+    def sibling_part(i):
+        return member_copy(part_out.at[i], part_in.at[i], part_send.at[i], part_recv.at[i], sibling)
+
+    across_part = member_copy(part_out.at[2], part_in.at[2], part_send.at[2], part_recv.at[2], across)
 
     for h in range(chunks):
         for d in steps:
             spread_copy(h, d).start()
     for d in range(1, m):
         pos_copy(d).start()
-        q_copy(d).start()
+    q_to_across.start()
+    q_to_sibling.start()
     posall[mg] = pos_ref[...]
 
     code_at = panel_blocks * lax.broadcasted_iota(jnp.int32, (query_blocks, panel_rows), 0) + (
@@ -275,6 +286,8 @@
         for d in steps:
             route_copy(0, h, d).start()
     routed[0, me] = stage[0, me]
+    q_to_across.wait_recv()
+    q_forward.start()
     for r in range(1, rounds):
         for c in range(n):
             for h in range(chunks):
@@ -287,7 +300,8 @@
 
     for d in range(1, m):
         pos_copy(d).wait_recv()
-        q_copy(d).wait_recv()
+    q_to_sibling.wait_recv()
+    q_forward.wait_recv()
 
     own = own_panel[...].reshape(panel_rows, columns)
     panel_row = lax.broadcasted_iota(jnp.int32, (panel_rows, rows), 0) + mg * panel_rows
@@ -344,13 +358,17 @@
 
             lax.fori_loop(0, m, query_block, 0)
         else:
-            def last_block(d, carry):
-                h = lax.rem(mg + d, m)
-                part_out[h] = (scale * (facc[h] + dot_nn(wbuf[h], panel))).astype(jnp.bfloat16)
-                part_copy(d).start()
+            def last_block(i, carry):
+                h = lax.rem(sibling + 2 * i, m)
+                part_out[i] = (scale * (facc[h] + dot_nn(wbuf[h], panel))).astype(jnp.bfloat16)
+                sibling_part(i).start()
                 return carry
 
-            lax.fori_loop(1, m, last_block, 0)
+            lax.fori_loop(0, 2, last_block, 0)
+            facc[across] = scale * (facc[across] + dot_nn(wbuf[across], panel))
+            sibling_part(1).wait_recv()
+            part_out[2] = (facc[across] + part_in[1].astype(jnp.float32)).astype(jnp.bfloat16)
+            across_part.start()
             qg_ref[...] = scale * (facc[mg] + dot_nn(wbuf[mg], panel))
 
     for r in range(rounds - 1):
@@ -376,9 +394,9 @@
             fin_copy(h, d).start()
     fin_in[me] = fin_out[me]
 
-    for d in range(1, m):
-        part_copy(d).wait_recv()
-        qg_ref[...] += part_in[lax.rem(mg + m - d, m)].astype(jnp.float32)
+    sibling_part(0).wait_recv()
+    across_part.wait_recv()
+    qg_ref[...] += part_in[0].astype(jnp.float32) + part_in[2].astype(jnp.float32)
 
     for h in range(chunks):
         for d in steps:
@@ -395,9 +413,9 @@
             for h in range(back_parts(r)):
                 back_copy(r, h, d).wait_send()
     for d in range(1, m):
-        q_copy(d).wait_send()
         pos_copy(d).wait_send()
-        part_copy(d).wait_send()
+    for copy in (q_to_across, q_to_sibling, q_forward, sibling_part(0), sibling_part(1), across_part):
+        copy.wait_send()
 
 
 def fused_shards(queries, passages, partner, pair_codes, pair_count, positive):
@@ -460,7 +478,7 @@
 
 def shards(queries, passages, partner, pair_codes, pair_count, positive):
     n = lax.axis_size("idx")
-    if passages.shape[1] % (32 * n) == 0 and partner.shape[1] == n:
+    if lax.axis_size("grp") == 4 and passages.shape[1] % (32 * n) == 0 and partner.shape[1] == n:
         return fused_shards(queries, passages, partner, pair_codes, pair_count, positive)
     return plain_shards(queries, passages, partner, pair_codes, pair_count, positive)
 

time: 67 us -> 66.9 us (level)
  no operation moved by 1% of the time
where the time goes in v4:
time: 66.9 us; the launch traced here: 66.7 us
  Pallas kernels  63.1 us (94%)
  local copies, waits for them, and re-layouts  3.02 us (5%)
    pallas_call x1, Pallas kernels, fused_shards(): pl.pallas_call(functools.partial(fused_kernel, n, m, rounds, columns ** (...  63.1 us
    unnamed x4, local copies, waits for them, and re-layouts  3.02 us

profile of v4, /device:TPU:0, one launch (start us, length us, event | category | flops | bytes accessed | tf_op | source)
XLA Modules:
  0.0 66.7 jit_solution(6755240538814077400)
XLA Ops:
  0.6 63.1 %shard_map.77 = (f32[256,768]{1,0:T(8,128)}, f32[256,768]{1,0:T(8,128)}) custom-call(s32[2,8]{1,0:T(2,128)} %partner_ref.1, s32[2,8,16]{2,1,0:T(8,128)} %bitcast.10, s32[2,8]{1,0:T(2,128)} %bitcast.11, bf16[256,768]{1,0:T(8,128)(2,1)} %bitcast.8, bf16[8,32,768]{2,1,0:T(8,128)(2,1)} %bitcast.9, s32[1,256]{1,0:T(1,128)} %pos_ref.1), custom_call_target="tpu_custom_call" | custom-call | tf_op jit(solution)/shard_map/pallas_call | solution.py:432
  63.7 0.0 copy-start
  63.7 2.1 %copy.10 = f32[1,256,768]{2,1,0:T(8,128)} copy(f32[1,256,768]{2,1,0:T(8,128)} %bitcast.7) | data formatting | bytes 1572864
  65.8 0.0 copy-done
  65.8 0.9 %copy.11 = f32[1,256,768]{2,1,0:T(8,128)} copy(f32[1,256,768]{2,1,0:T(8,128)S(1)} %bitcast.6) | data formatting | bytes 1572864
Async XLA Ops:
  63.7 2.1 %copy-start = (f32[256,768]{1,0:T(8,128)S(1)}, f32[256,768]{1,0:T(8,128)}, u32[]{:S(2)}) copy-start(f32[256,768]{1,0:T(8,128)} %get-tuple-element.5) | copy-start | bytes 2359300

commit v5 on v4

--- a/solution.py
+++ b/solution.py
@@ -293,8 +293,6 @@
             for h in range(chunks):
                 stage[r, c, part_rows(h, chunks)] = spread[h][partner_ref[r, c]]
         for d in steps:
-            for h in range(route_parts(r - 1)):
-                route_copy(r - 1, h, d).wait_send()
             route_copy(r, 0, d).start()
         routed[r, me] = stage[r, me]
 
@@ -407,9 +405,9 @@
         for h in range(chunks):
             spread_copy(h, d).wait_send()
             fin_copy(h, d).wait_send()
-        for h in range(route_parts(rounds - 1)):
-            route_copy(rounds - 1, h, d).wait_send()
         for r in range(rounds):
+            for h in range(route_parts(r)):
+                route_copy(r, h, d).wait_send()
             for h in range(back_parts(r)):
                 back_copy(r, h, d).wait_send()
     for d in range(1, m):

time: 66.9 us -> 66.9 us (level)
  no operation moved by 1% of the time
where the time goes in v5:
time: 66.9 us; the launch traced here: 66.7 us
  Pallas kernels  63 us (94%)
  local copies, waits for them, and re-layouts  3.02 us (5%)
    pallas_call x1, Pallas kernels, fused_shards(): pl.pallas_call(functools.partial(fused_kernel, n, m, rounds, columns ** (...  63 us
    unnamed x4, local copies, waits for them, and re-layouts  3.02 us

profile of v5, /device:TPU:0, one launch (start us, length us, event | category | flops | bytes accessed | tf_op | source)
XLA Modules:
  0.0 66.7 jit_solution(2669599774235963421)
XLA Ops:
  0.6 63.0 %shard_map.77 = (f32[256,768]{1,0:T(8,128)}, f32[256,768]{1,0:T(8,128)}) custom-call(s32[2,8]{1,0:T(2,128)} %partner_ref.1, s32[2,8,16]{2,1,0:T(8,128)} %bitcast.10, s32[2,8]{1,0:T(2,128)} %bitcast.11, bf16[256,768]{1,0:T(8,128)(2,1)} %bitcast.8, bf16[8,32,768]{2,1,0:T(8,128)(2,1)} %bitcast.9, s32[1,256]{1,0:T(1,128)} %pos_ref.1), custom_call_target="tpu_custom_call" | custom-call | tf_op jit(solution)/shard_map/pallas_call | solution.py:430
  63.7 0.0 copy-start
  63.7 2.1 %copy.10 = f32[1,256,768]{2,1,0:T(8,128)} copy(f32[1,256,768]{2,1,0:T(8,128)} %bitcast.7) | data formatting | bytes 1572864
  65.8 0.0 copy-done
  65.8 0.9 %copy.11 = f32[1,256,768]{2,1,0:T(8,128)} copy(f32[1,256,768]{2,1,0:T(8,128)S(1)} %bitcast.6) | data formatting | bytes 1572864
Async XLA Ops:
  63.7 2.1 %copy-start = (f32[256,768]{1,0:T(8,128)S(1)}, f32[256,768]{1,0:T(8,128)}, u32[]{:S(2)}) copy-start(f32[256,768]{1,0:T(8,128)} %get-tuple-element.5) | copy-start | bytes 2359300
